TPU v7x, 512 devices: a whole 4x4x16 slice. The times are simulated.
512 devices in a mesh: dp: 4 (over z_hi), cin: 32 (over y, x, core), cout: 4 (over z_lo).
Axes of the slice: x: 4, y: 4, z: 16 (z_hi: 4, z_lo: 4; z = z_hi * 4 + z_lo), core: 2. Of those that a mesh axis runs over, the one named last changes fastest.
Arguments:
- weight: bfloat16 [8, 2, 2048, 2048], P(None, None, 'cin', 'cout'), may hold values from -0.09375 to 0.09375
- spectrum: bfloat16 [8, 2, 2048, 2048], P(None, None, ('cin', 'cout'), 'dp'), may hold values from -0.1796875 to 0.1796875
- out_grad: bfloat16 [8, 2, 2048, 2048], P(None, None, ('cout', 'cin'), 'dp'), may hold values from -6 to 6
Outputs:
- spectrum_grad: bfloat16 [8, 2, 2048, 2048], P(None, None, ('cin', 'cout'), 'dp')
- weight_grad: bfloat16 [8, 2, 2048, 2048], P(None, None, 'cin', 'cout')
All inputs are finite; a program needn't handle non-finite values.
Results may differ from a plain program's by a relative error of at most 0.001.
Values may be sent and summed in bfloat16 or wider, within the bound.
No kernel may reach another device: no remote copies, remote signals or barrier semaphores. Data moves between devices by JAX's collectives and lax.ppermute only.
A program may use at most 64 MiB of HBM per device.

v0:
```python
import jax
import jax.numpy as jnp
from jax import lax
from jax.sharding import PartitionSpec as P


def block_terms(columns, rows_in, piece):
    w_real = columns[:, 0]
    w_imag = columns[:, 1]
    g_real = piece[:, 0]
    g_imag = piece[:, 1]
    x_real = rows_in[:, 0]
    x_imag = rows_in[:, 1]
    dx_real = jnp.einsum(
        "mio,mob->mib", w_real, g_real, preferred_element_type=jnp.float32
    ) + jnp.einsum("mio,mob->mib", w_imag, g_imag, preferred_element_type=jnp.float32)
    dx_imag = jnp.einsum(
        "mio,mob->mib", w_real, g_imag, preferred_element_type=jnp.float32
    ) - jnp.einsum("mio,mob->mib", w_imag, g_real, preferred_element_type=jnp.float32)
    dw_real = jnp.einsum(
        "mib,mob->mio", x_real, g_real, preferred_element_type=jnp.float32
    ) + jnp.einsum("mib,mob->mio", x_imag, g_imag, preferred_element_type=jnp.float32)
    dw_imag = jnp.einsum(
        "mib,mob->mio", x_real, g_imag, preferred_element_type=jnp.float32
    ) - jnp.einsum("mib,mob->mio", x_imag, g_real, preferred_element_type=jnp.float32)
    return (jnp.stack([dx_real, dx_imag], axis=1), jnp.stack([dw_real, dw_imag], axis=1))


def accumulate(weight, rows_in, grads):
    part_in, block = block_terms(weight, rows_in, lax.all_gather(grads, "cin", axis=2, tiled=True))
    return (part_in, block)


def on_device(weight, spectrum, out_grad):
    rows_in = lax.all_gather(spectrum, "cout", axis=2, tiled=True)
    term_in, term_weight = accumulate(weight, rows_in, out_grad)
    summed = lax.psum(term_weight, "dp")
    weight_grad = summed.astype(jnp.bfloat16)
    spectrum_grad = lax.psum_scatter(term_in, "cout", scatter_dimension=2, tiled=True).astype(
        jnp.bfloat16
    )
    return (spectrum_grad, weight_grad)


def solution(mesh):
    placed = (
        P(None, None, "cin", "cout"),
        P(None, None, ("cin", "cout"), "dp"),
        P(None, None, ("cout", "cin"), "dp"),
    )
    return jax.shard_map(
        on_device,
        mesh=mesh,
        in_specs=placed,
        out_specs=(P(None, None, ("cin", "cout"), "dp"), P(None, None, "cin", "cout")),
        check_vma=False,
    )
```

profile of v0, /device:TPU:34, one launch (start us, length us, event | category | flops | bytes accessed | tf_op | source)
XLA Modules:
  0.0 329.4 jit_solution(9001423755656557211)
XLA Ops:
  7.2 0.0 copy-start.1
  7.2 0.0 all-gather.3.cloned.1.call-start
  7.2 1.7 copy.6
  9.0 0.0 all-gather.3.cloned.1.call-update
  9.0 0.0 all-gather.5.cloned.1.call-start
  9.0 1.7 copy.8
  10.7 0.0 all-gather.5.cloned.1.call-update
  10.7 0.0 reduce-scatter.2.cloned.1.call-start
  10.8 73.4 %all-gather.3.cloned.1.call-done = bf16[8,2,512,512]{3,2,0,1:T(8,128)(2,1)} async-done(((bf16[8,2,16,512]{3,2,0,1:T(8,128)(2,1)}), bf16[8,2,512,512]{3,2,0,1:T(8,128)(2,1)}) %all-gather.3.cloned.1.call-update) | async-done | bytes 8388624 | tf_op jit(solution)/shard_map/all_gather | solution.py:30
  84.2 0.0 copy-start
  84.2 3.3 %fusion.3 = f32[8,64,512]{2,1,0:T(8,128)S(1)} fusion(bf16[8,2,512,512]{3,2,0,1:T(8,128)(2,1)} %all-gather.3.cloned.1.call-done, bf16[8,2,64,512]{3,2,1,0:T(8,128)(2,1)} %param.3), kind=kOutput, calls=%fused_computation.5 | convolution fusion | flops 268435456 | bytes 5767168 | tf_op jit(solution)/shard_map/mio,mob->mib/dot_general | solution.py:14
  87.5 0.0 copy-done.1
  87.5 3.5 %fusion.2 = f32[8,64,512]{2,1,0:T(8,128)S(1)} fusion(bf16[8,2,512,512]{3,2,0,1:T(8,128)(2,1)} %all-gather.3.cloned.1.call-done, bf16[8,2,64,512]{3,2,1,0:T(8,128)(2,1)S(1)} %copy-done.1), kind=kOutput, calls=%fused_computation.4 | convolution fusion | flops 268435456 | bytes 5767168 | tf_op jit(solution)/shard_map/mio,mob->mib/dot_general | solution.py:19
  91.0 0.0 copy-done
  91.0 0.8 fusion.9
  91.8 0.8 fusion.11
  92.6 1.5 pad_maximum_fusion
  94.1 0.0 reduce-scatter.2.cloned.1.call-update
  94.1 29.1 %all-gather.5.cloned.1.call-done = bf16[8,2,64,512]{3,2,0,1:T(8,128)(2,1)} async-done(((bf16[8,2,16,512]{3,2,0,1:T(8,128)(2,1)}), bf16[8,2,64,512]{3,2,0,1:T(8,128)(2,1)}) %all-gather.5.cloned.1.call-update) | async-done | bytes 1048592 | tf_op jit(solution)/shard_map/all_gather | solution.py:35
  123.2 0.0 copy-start.2
  123.2 0.0 slice-start
  123.2 3.9 %fusion.1 = f32[8,64,512]{2,1,0:T(8,128)S(1)} fusion(bf16[8,2,512,512]{3,2,0,1:T(8,128)(2,1)} %all-gather.3.cloned.1.call-done, bf16[8,2,64,512]{3,2,0,1:T(8,128)(2,1)} %all-gather.5.cloned.1.call-done), kind=kOutput, calls=%fused_computation.3 | convolution fusion | flops 268435456 | bytes 5767168 | tf_op jit(solution)/shard_map/mib,mob->mio/dot_general | solution.py:20
  127.1 0.0 copy-done.2
  127.1 0.0 slice-start.1
  127.1 3.7 %fusion = f32[8,64,512]{2,1,0:T(8,128)S(1)} fusion(bf16[8,2,512,512]{3,2,0,1:T(8,128)(2,1)} %all-gather.3.cloned.1.call-done, bf16[8,2,64,512]{3,2,0,1:T(8,128)(2,1)S(1)} %copy-done.2), kind=kOutput, calls=%fused_computation.2 | convolution fusion | flops 268435456 | bytes 5767168 | tf_op jit(solution)/shard_map/mib,mob->mio/dot_general | solution.py:25
  130.8 3.6 %fusion.13 = f32[8,1,64,512]{3,2,0,1:T(8,128)S(1)} fusion(f32[8,64,512]{2,1,0:T(8,128)S(1)} %fusion.1, bf16[8,2,512,512]{3,2,0,1:T(8,128)(2,1)} %all-gather.3.cloned.1.call-done, bf16[8,2,64,512]{3,2,0,1:T(8,128)(2,1)S(1)} %copy-done.2), kind=kOutput, calls=%fused_computation.17 | convolution fusion | flops 268697600 | bytes 6815744 | tf_op jit(solution)/shard_map/mib,mob->mio/dot_general | solution.py:22
  134.4 0.0 slice-done
  134.4 0.0 slice-done.1
  134.4 1.4 fusion.15
  135.8 0.2 pad_maximum_fusion.1
  136.0 184.0 %all-reduce.1 = bf16[8,2,64,512]{3,2,0,1:T(8,128)(2,1)S(1)} all-reduce(f32[8,2,64,512]{3,2,0,1:T(8,128)S(1)} %pad_maximum_fusion.1), channel_id=1, replica_groups=mesh['dp'=4,'cin'=32,'cout'=4] {'dp'}, use_global_device_ids=true, to_apply=%region_1.0 | all-reduce | flops 524288 | bytes 3145728 | tf_op jit(solution)/shard_map/psum | solution.py:37
  320.1 1.1 copy.10
  321.1 0.0 reduce-scatter.2.cloned.1.call-done
  321.1 1.1 convert_element_type.6
  322.2 0.7 copy.9
  (1 shorter events, 0.0 us)
Async XLA Ops:
  7.2 80.3 %copy-start.1 = (bf16[8,2,64,512]{3,2,1,0:T(8,128)(2,1)S(1)}, bf16[8,2,64,512]{3,2,1,0:T(8,128)(2,1)}, u32[]{:S(2)}) copy-start(bf16[8,2,64,512]{3,2,1,0:T(8,128)(2,1)} %param.3) | copy-start | bytes 3145732
  7.2 77.0 %all-gather.3.cloned.1.call-start = ((), (), s32[]{:S(2)}) async-start(), calls=%async_computation.1 | async-start | bytes 8650752 | tf_op jit(solution)/shard_map/all_gather | solution.py:30
  9.0 114.2 %all-gather.5.cloned.1.call-start = ((), (), s32[]{:S(2)}) async-start(), calls=%async_computation.3 | async-start | bytes 1310720 | tf_op jit(solution)/shard_map/all_gather | solution.py:35
  10.7 310.4 %reduce-scatter.2.cloned.1.call-start = ((), (), s32[]{:S(2)}) async-start(), calls=%async_computation.2 | async-start | bytes 2621440 | tf_op jit(solution)/shard_map/reduce_scatter | solution.py:39
  84.2 6.8 %copy-start = (bf16[8,2,512,512]{3,2,0,1:T(8,128)(2,1)S(1)}, bf16[8,2,512,512]{3,2,0,1:T(8,128)(2,1)}, u32[]{:S(2)}) copy-start(bf16[8,2,512,512]{3,2,0,1:T(8,128)(2,1)} %all-gather.3.cloned.1.call-done) | copy-start | bytes 25165828
  123.2 3.9 %copy-start.2 = (bf16[8,2,64,512]{3,2,0,1:T(8,128)(2,1)S(1)}, bf16[8,2,64,512]{3,2,0,1:T(8,128)(2,1)}, u32[]{:S(2)}) copy-start(bf16[8,2,64,512]{3,2,0,1:T(8,128)(2,1)} %all-gather.5.cloned.1.call-done) | copy-start | bytes 3145732
  123.2 11.2 %slice-start = ((s8[8388608]{0:T(1024)(128)(4,1)}), s8[4194304]{0:T(1024)(128)(4,1)S(1)}, s32[]{:S(2)}) async-start(s8[8388608]{0:T(1024)(128)(4,1)} %bitcast.58), calls=%async_computation.4 | async-start | bytes 8388608
  127.1 7.3 %slice-start.1 = ((s8[8388608]{0:T(1024)(128)(4,1)}), s8[4194304]{0:T(1024)(128)(4,1)S(1)}, s32[]{:S(2)}) async-start(s8[8388608]{0:T(1024)(128)(4,1)} %bitcast.58), calls=%async_computation.5 | async-start | bytes 8388608
Sparse Core Ops, SparseCore 0:
  11.8 72.3 all-gather.2
  86.8 36.3 all-gather.4
  126.0 147.0 reduce-scatter.1
where the time goes:
time: 330 us; the launch traced here: 329 us
  blocking collectives  184 us (56%)
  waiting for transfers between devices  102 us (31%)
  matrix products  20.9 us (6%)
  between operations  13.9 us (4%)
  local copies, waits for them, and re-layouts  5.23 us (2%)
    psum x1, blocking collectives, on_device(): summed = lax.psum(term_weight, 'dp')  184 us
    all_gather x1, waiting for transfers between devices, accumulate(): lax.all_gather(grads, 'cin', axis=2, tiled=True)  73.4 us
    all_gather x1, waiting for transfers between devices, on_device(): rows_in = lax.all_gather(spectrum, 'cout', axis=2, tiled=True)  29.1 us
  transfers between devices with their start and end apart: 3, of which 2 were waited for; matrix products, arithmetic and copies ran while one was open for 8% of the time, Pallas kernels for 0%

commit v1 on v0

--- a/solution.py
+++ b/solution.py
@@ -2,6 +2,10 @@
 import jax.numpy as jnp
 from jax import lax
 from jax.sharding import PartitionSpec as P
+
+_compute_frame = lambda page: jnp.concatenate(
+    lax.all_to_all(jnp.stack([page for _ in range(lax.axis_size("cin"))]), "cin", 0, 0), axis=2
+)
 
 
 def block_terms(columns, rows_in, piece):
@@ -27,7 +31,7 @@
 
 
 def accumulate(weight, rows_in, grads):
-    part_in, block = block_terms(weight, rows_in, lax.all_gather(grads, "cin", axis=2, tiled=True))
+    part_in, block = block_terms(weight, rows_in, _compute_frame(grads))
     return (part_in, block)
 
 

time: 330 us -> 351 us (1.064)
  the two profiles are of different devices: /device:TPU:34 before, /device:TPU:64 now
where the time goes in v1:
time: 351 us
  blocking collectives  184 us (52%)
  waiting for transfers between devices  105 us (30%)
  matrix products  20.8 us (6%)
  local copies, waits for them, and re-layouts  15.9 us (5%)
  between operations  14.2 us (4%)
  starting transfers between devices  7.66 us (2%)
    psum x1, blocking collectives, on_device(): summed = lax.psum(term_weight, 'dp')  184 us
    all_to_all x1, waiting for transfers between devices, lax.all_to_all(jnp.stack([page for _ in range(lax.axis_size('cin'))]), 'c...  105 us
    reshape x1, local copies, waits for them, and re-layouts, jnp.concatenate(lax.all_to_all(jnp.stack([page for _ in range(lax.axis_si...  8.09 us
    all_to_all x1, starting transfers between devices, lax.all_to_all(jnp.stack([page for _ in range(lax.axis_size('cin'))]), 'c...  7.58 us
  transfers between devices with their start and end apart: 3, of which 1 were waited for; matrix products, arithmetic and copies ran while one was open for 9% of the time, Pallas kernels for 0%

profile of v1, /device:TPU:64, one launch (start us, length us, event | category | flops | bytes accessed | tf_op | source)
XLA Modules:
  0.0 350.7 jit_solution(12308804920906341240)
XLA Ops:
  7.2 1.0 copy.12
  8.1 4.3 %stack.14 = bf16[32,8,2,16,512]{4,3,1,2,0:T(8,128)(2,1)} broadcast(bf16[8,2,16,512]{3,2,0,1:T(8,128)(2,1)S(1)} %copy.12), dimensions={1,2,3,4} | broadcast | bytes 8650752 | tf_op jit(solution)/shard_map/stack | solution.py:7
  12.4 0.0 copy-start.3
  12.4 7.6 %all-to-all-start = ((bf16[32,8,2,16,512]{4,3,1,2,0:T(8,128)(2,1)}), bf16[32,8,2,16,512]{4,3,1,2,0:T(8,128)(2,1)}, u32[]{:S(2)}, u32[]{:S(2)}) async-start(bf16[32,8,2,16,512]{4,3,1,2,0:T(8,128)(2,1)} %stack.14), calls=%async_computation | async-start | bytes 16777216 | tf_op jit(solution)/shard_map/all_to_all | solution.py:7
  20.0 0.0 all-gather.2.cloned.1.call-start
  20.1 0.0 copy-done.3
  20.1 0.7 copy.15
  20.8 0.0 all-gather.2.cloned.1.call-update
  20.8 0.0 reduce-scatter.2.cloned.1.call-start
  20.9 105.0 %all-to-all-done = bf16[32,8,2,16,512]{4,3,1,2,0:T(8,128)(2,1)} async-done(((bf16[32,8,2,16,512]{4,3,1,2,0:T(8,128)(2,1)}), bf16[32,8,2,16,512]{4,3,1,2,0:T(8,128)(2,1)}, u32[]{:S(2)}, u32[]{:S(2)}) %all-to-all-start) | async-done | bytes 8388640 | tf_op jit(solution)/shard_map/all_to_all | solution.py:7
  125.9 0.0 copy-start.1
  125.9 8.1 %copy.13 = bf16[8,2,32,16,512]{4,3,2,0,1:T(8,128)(2,1)} copy(bf16[8,2,32,16,512]{4,3,0,1,2:T(8,128)(2,1)} %bitcast.1) | data formatting | bytes 16777216 | tf_op jit(solution)/shard_map/reshape | solution.py:6
  134.0 0.0 copy-done.1
  134.0 0.0 copy-start
  134.0 3.2 fusion.3
  137.2 3.5 fusion.2
  140.7 0.0 copy-done
  140.7 0.8 fusion.9
  141.5 0.8 fusion.11
  142.3 1.5 pad_maximum_fusion
  143.8 0.0 reduce-scatter.2.cloned.1.call-update
  143.8 0.0 all-gather.2.cloned.1.call-done
  143.9 0.0 copy-start.2
  143.9 0.0 slice-start
  143.9 3.9 %fusion.1 = f32[8,64,512]{2,1,0:T(8,128)S(1)} fusion(bf16[8,2,512,512]{3,2,0,1:T(8,128)(2,1)} %bitcast.62, bf16[8,2,64,512]{3,2,0,1:T(8,128)(2,1)} %all-gather.2.cloned.1.call-done), kind=kOutput, calls=%fused_computation.3 | convolution fusion | flops 268435456 | bytes 5767168 | tf_op jit(solution)/shard_map/mib,mob->mio/dot_general | solution.py:24
  147.7 0.0 copy-done.2
  147.8 0.0 slice-start.1
  147.8 3.7 %fusion = f32[8,64,512]{2,1,0:T(8,128)S(1)} fusion(bf16[8,2,512,512]{3,2,0,1:T(8,128)(2,1)} %bitcast.63, bf16[8,2,64,512]{3,2,0,1:T(8,128)(2,1)S(1)} %copy-done.2), kind=kOutput, calls=%fused_computation.2 | convolution fusion | flops 268435456 | bytes 5767168 | tf_op jit(solution)/shard_map/mib,mob->mio/dot_general | solution.py:29
  151.5 3.6 %fusion.13 = f32[8,1,64,512]{3,2,0,1:T(8,128)S(1)} fusion(f32[8,64,512]{2,1,0:T(8,128)S(1)} %fusion.1, bf16[8,2,512,512]{3,2,0,1:T(8,128)(2,1)} %bitcast.64, bf16[8,2,64,512]{3,2,0,1:T(8,128)(2,1)S(1)} %copy-done.2), kind=kOutput, calls=%fused_computation.17 | convolution fusion | flops 268697600 | bytes 6815744 | tf_op jit(solution)/shard_map/mib,mob->mio/dot_general | solution.py:26
  155.0 0.0 slice-done
  155.1 0.0 slice-done.1
  155.1 1.4 fusion.15
  156.4 0.2 pad_maximum_fusion.1
  156.7 184.3 %all-reduce.1 = bf16[8,2,64,512]{3,2,0,1:T(8,128)(2,1)S(1)} all-reduce(f32[8,2,64,512]{3,2,0,1:T(8,128)S(1)} %pad_maximum_fusion.1), channel_id=1, replica_groups=mesh['dp'=4,'cin'=32,'cout'=4] {'dp'}, use_global_device_ids=true, to_apply=%region_1.0 | all-reduce | flops 524288 | bytes 3145728 | tf_op jit(solution)/shard_map/psum | solution.py:41
  341.0 1.1 copy.17
  342.1 0.0 reduce-scatter.2.cloned.1.call-done
  342.1 1.1 convert_element_type.6
  343.2 0.7 copy.16
  (1 shorter events, 0.0 us)
Async XLA Ops:
  12.4 7.6 %copy-start.3 = (bf16[8,2,16,512]{3,2,1,0:T(8,128)(2,1)S(1)}, bf16[8,2,16,512]{3,2,1,0:T(8,128)(2,1)}, u32[]{:S(2)}) copy-start(bf16[8,2,16,512]{3,2,1,0:T(8,128)(2,1)} %param.4) | copy-start | bytes 786436
  12.4 113.5 %all-to-all-start = ((bf16[32,8,2,16,512]{4,3,1,2,0:T(8,128)(2,1)}), bf16[32,8,2,16,512]{4,3,1,2,0:T(8,128)(2,1)}, u32[]{:S(2)}, u32[]{:S(2)}) async-start(bf16[32,8,2,16,512]{4,3,1,2,0:T(8,128)(2,1)} %stack.14), calls=%async_computation | async-start | bytes 16777216 | tf_op jit(solution)/shard_map/all_to_all | solution.py:7
  20.0 123.8 %all-gather.2.cloned.1.call-start = ((), (), s32[]{:S(2)}) async-start(), calls=%async_computation.3 | async-start | bytes 1310720 | tf_op jit(solution)/shard_map/all_gather | solution.py:39
  20.8 321.3 %reduce-scatter.2.cloned.1.call-start = ((), (), s32[]{:S(2)}) async-start(), calls=%async_computation.2 | async-start | bytes 2621440 | tf_op jit(solution)/shard_map/reduce_scatter | solution.py:43
  125.9 8.1 %copy-start.1 = (bf16[8,2,64,512]{3,2,1,0:T(8,128)(2,1)S(1)}, bf16[8,2,64,512]{3,2,1,0:T(8,128)(2,1)}, u32[]{:S(2)}) copy-start(bf16[8,2,64,512]{3,2,1,0:T(8,128)(2,1)} %param.3) | copy-start | bytes 3145732
  134.0 6.7 %copy-start = (bf16[8,2,32,16,512]{4,3,2,0,1:T(8,128)(2,1)S(1)}, bf16[8,2,32,16,512]{4,3,2,0,1:T(8,128)(2,1)}, u32[]{:S(2)}) copy-start(bf16[8,2,32,16,512]{4,3,2,0,1:T(8,128)(2,1)} %copy.13) | copy-start | bytes 25165828
  143.9 3.9 %copy-start.2 = (bf16[8,2,64,512]{3,2,0,1:T(8,128)(2,1)S(1)}, bf16[8,2,64,512]{3,2,0,1:T(8,128)(2,1)}, u32[]{:S(2)}) copy-start(bf16[8,2,64,512]{3,2,0,1:T(8,128)(2,1)} %all-gather.2.cloned.1.call-done) | copy-start | bytes 3145732
  143.9 11.2 %slice-start = ((s8[8388608]{0:T(1024)(128)(4,1)}), s8[4194304]{0:T(1024)(128)(4,1)S(1)}, s32[]{:S(2)}) async-start(s8[8388608]{0:T(1024)(128)(4,1)} %bitcast.67), calls=%async_computation.4 | async-start | bytes 8388608
  147.8 7.3 %slice-start.1 = ((s8[8388608]{0:T(1024)(128)(4,1)}), s8[4194304]{0:T(1024)(128)(4,1)S(1)}, s32[]{:S(2)}) async-start(s8[8388608]{0:T(1024)(128)(4,1)} %bitcast.67), calls=%async_computation.5 | async-start | bytes 8388608
Sparse Core Ops, SparseCore 0:
  23.5 40.8 all-gather.1
  143.9 142.0 reduce-scatter.1

commit v2 on v0

--- a/solution.py
+++ b/solution.py
@@ -2,6 +2,12 @@
 import jax.numpy as jnp
 from jax import lax
 from jax.sharding import PartitionSpec as P
+
+
+def add_all(shard, mesh_axis):
+    blocks = lax.all_gather(shard, mesh_axis, axis=0, tiled=False)
+    total = blocks.sum(axis=0)
+    return total
 
 
 def block_terms(columns, rows_in, piece):
@@ -34,7 +40,7 @@
 def on_device(weight, spectrum, out_grad):
     rows_in = lax.all_gather(spectrum, "cout", axis=2, tiled=True)
     term_in, term_weight = accumulate(weight, rows_in, out_grad)
-    summed = lax.psum(term_weight, "dp")
+    summed = add_all(term_weight, "dp")
     weight_grad = summed.astype(jnp.bfloat16)
     spectrum_grad = lax.psum_scatter(term_in, "cout", scatter_dimension=2, tiled=True).astype(
         jnp.bfloat16

time: 330 us -> 496 us (1.50)
  the two profiles are of different devices: /device:TPU:34 before, /device:TPU:1 now
where the time goes in v2:
time: 496 us
  waiting for transfers between devices  447 us (90%)
  matrix products  20.9 us (4%)
  between operations  13.9 us (3%)
  other arithmetic  8.81 us (2%)
  local copies, waits for them, and re-layouts  5.23 us (1%)
    all_gather x1, waiting for transfers between devices, add_all(): blocks = lax.all_gather(shard, mesh_axis, axis=0, tiled=False)  299 us
    all_gather x1, waiting for transfers between devices, accumulate(): lax.all_gather(grads, 'cin', axis=2, tiled=True)  75 us
    reduce_scatter x1, waiting for transfers between devices, on_device(): lax.psum_scatter(term_in, 'cout', scatter_dimension=2, tiled=True)  42 us
    all_gather x1, waiting for transfers between devices, on_device(): rows_in = lax.all_gather(spectrum, 'cout', axis=2, tiled=True)  30.4 us
  transfers between devices with their start and end apart: 4, of which 4 were waited for; matrix products, arithmetic and copies ran while one was open for 6% of the time, Pallas kernels for 0%

profile of v2, /device:TPU:1, one launch (start us, length us, event | category | flops | bytes accessed | tf_op | source)
XLA Modules:
  0.0 495.9 jit_solution(13762476108574822858)
XLA Ops:
  7.2 0.0 copy-start.1
  7.2 0.0 all-gather.5.cloned.1.call-start
  7.2 1.7 copy.11
  9.0 0.0 all-gather.5.cloned.1.call-update
  9.0 0.0 all-gather.7.cloned.1.call-start
  9.0 1.7 copy.13
  10.7 0.0 all-gather.7.cloned.1.call-update
  10.7 0.0 reduce-scatter.2.cloned.1.call-start
  10.8 75.0 %all-gather.5.cloned.1.call-done = bf16[8,2,512,512]{3,2,0,1:T(8,128)(2,1)} async-done(((bf16[8,2,16,512]{3,2,0,1:T(8,128)(2,1)}), bf16[8,2,512,512]{3,2,0,1:T(8,128)(2,1)}) %all-gather.5.cloned.1.call-update) | async-done | bytes 8388624 | tf_op jit(solution)/shard_map/all_gather | solution.py:36
  85.8 0.0 copy-start
  85.8 3.3 fusion.2
  89.1 0.0 copy-done.1
  89.1 3.5 fusion.3
  92.6 0.0 copy-done
  92.6 0.8 fusion.11
  93.4 0.8 fusion.9
  94.2 1.5 pad_maximum_fusion
  95.8 0.0 reduce-scatter.2.cloned.1.call-update
  95.8 0.0 all-gather.9.cloned.1.call-start
  95.8 30.4 %all-gather.7.cloned.1.call-done = bf16[8,2,64,512]{3,2,0,1:T(8,128)(2,1)} async-done(((bf16[8,2,16,512]{3,2,0,1:T(8,128)(2,1)}), bf16[8,2,64,512]{3,2,0,1:T(8,128)(2,1)}) %all-gather.7.cloned.1.call-update) | async-done | bytes 1048592 | tf_op jit(solution)/shard_map/all_gather | solution.py:41
  126.2 0.0 copy-start.2
  126.2 0.0 slice-start
  126.2 3.9 fusion
  130.1 0.0 copy-done.2
  130.1 0.0 slice-start.1
  130.1 3.7 fusion.1
  133.8 3.6 fusion.15
  137.4 0.0 slice-done
  137.4 0.0 slice-done.1
  137.4 1.4 fusion.13
  138.8 1.6 pad_maximum_fusion.1
  140.4 0.0 all-gather.9.cloned.1.call-update
  140.4 42.0 %reduce-scatter.2.cloned.1.call-done = f32[8,2,16,512]{3,2,0,1:T(8,128)} async-done(((f32[8,2,64,512]{3,2,0,1:T(8,128)}), f32[8,2,16,512]{3,2,0,1:T(8,128)}) %reduce-scatter.2.cloned.1.call-update) | async-done | bytes 524304 | tf_op jit(solution)/shard_map/reduce_scatter | solution.py:45
  182.5 1.1 convert_element_type.6
  183.5 0.7 copy.14
  184.3 299.5 %all-gather.9.cloned.1.call-done = f32[32,2,64,512]{3,2,0,1:T(8,128)} async-done(((f32[8,2,64,512]{3,2,0,1:T(8,128)}), f32[32,2,64,512]{3,2,0,1:T(8,128)}) %all-gather.9.cloned.1.call-update) | async-done | bytes 8388624 | tf_op jit(solution)/shard_map/all_gather | solution.py:8
  483.7 4.6 reduce_sum.9
  488.3 1.1 copy.15
  (1 shorter events, 0.0 us)
Async XLA Ops:
  7.2 82.0 %copy-start.1 = (bf16[8,2,64,512]{3,2,1,0:T(8,128)(2,1)S(1)}, bf16[8,2,64,512]{3,2,1,0:T(8,128)(2,1)}, u32[]{:S(2)}) copy-start(bf16[8,2,64,512]{3,2,1,0:T(8,128)(2,1)} %param.3) | copy-start | bytes 3145732
  7.2 78.6 %all-gather.5.cloned.1.call-start = ((), (), s32[]{:S(2)}) async-start(), calls=%async_computation.1 | async-start | bytes 8650752 | tf_op jit(solution)/shard_map/all_gather | solution.py:36
  9.0 117.2 %all-gather.7.cloned.1.call-start = ((), (), s32[]{:S(2)}) async-start(), calls=%async_computation.3 | async-start | bytes 1310720 | tf_op jit(solution)/shard_map/all_gather | solution.py:41
  10.7 171.7 %reduce-scatter.2.cloned.1.call-start = ((), (), s32[]{:S(2)}) async-start(), calls=%async_computation.2 | async-start | bytes 2621440 | tf_op jit(solution)/shard_map/reduce_scatter | solution.py:45
  85.8 6.8 %copy-start = (bf16[8,2,512,512]{3,2,0,1:T(8,128)(2,1)S(1)}, bf16[8,2,512,512]{3,2,0,1:T(8,128)(2,1)}, u32[]{:S(2)}) copy-start(bf16[8,2,512,512]{3,2,0,1:T(8,128)(2,1)} %all-gather.5.cloned.1.call-done) | copy-start | bytes 25165828
  95.8 387.9 %all-gather.9.cloned.1.call-start = ((), (), s32[]{:S(2)}) async-start(), calls=%async_computation.4 | async-start | bytes 10485760 | tf_op jit(solution)/shard_map/all_gather | solution.py:8
  126.2 3.9 copy-start.2
  126.2 11.2 %slice-start = ((s8[8388608]{0:T(1024)(128)(4,1)}), s8[4194304]{0:T(1024)(128)(4,1)S(1)}, s32[]{:S(2)}) async-start(s8[8388608]{0:T(1024)(128)(4,1)} %bitcast.59), calls=%async_computation.5 | async-start | bytes 8388608
  130.1 7.3 %slice-start.1 = ((s8[8388608]{0:T(1024)(128)(4,1)}), s8[4194304]{0:T(1024)(128)(4,1)S(1)}, s32[]{:S(2)}) async-start(s8[8388608]{0:T(1024)(128)(4,1)} %bitcast.59), calls=%async_computation.6 | async-start | bytes 8388608
Sparse Core Ops, SparseCore 0:
  11.8 73.9 all-gather.4
  88.5 37.6 all-gather.6
  129.1 53.3 reduce-scatter.1
  184.6 299.0 all-gather.8
